TPU v7x, 512 devices: a whole 4x4x16 slice. The times are simulated.
512 devices in a mesh: gx: 64 (over z, x_lo, core), gy: 8 (over y, x_hi).
Axes of the slice: x: 4 (x_hi: 2, x_lo: 2; x = x_hi * 2 + x_lo), y: 4, z: 16, core: 2. Of those that a mesh axis runs over, the one named last changes fastest.
Arguments:
- grad_late: float32 [2, 20, 512, 1024], P(None, None, 'gx', 'gy'), may hold values from -6 to 6
- grad_early: float32 [2, 20, 512, 1024], P(None, None, 'gx', 'gy'), may hold values from -6 to 6
- accumulation: bfloat16 [4, 20, 512, 1024], P(None, None, 'gx', 'gy'), may hold values from -0.021 to 0.302, as said below
- mobility_late: bfloat16 [4, 20, 512, 1024], P(None, None, 'gx', 'gy'), may hold values from -0.25 to 1.4, as said below
- mobility_early: bfloat16 [4, 20, 512, 1024], P(None, None, 'gx', 'gy'), may hold values from -0.25 to 1.4, as said below
- trans_x: bfloat16 [20, 512, 1024], P(None, 'gx', 'gy'), may hold values from 0.0099487305 to 1
- trans_y: bfloat16 [20, 512, 1024], P(None, 'gx', 'gy'), may hold values from 0.0099487305 to 1
- trans_z: bfloat16 [20, 512, 1024], P(None, 'gx', 'gy'), may hold values from 0.0099487305 to 1
- perf_cell: int32 [64, 8, 256], P('gx', 'gy'), may hold values from 0 to 20479
- perf_well: int32 [64, 8, 256], P('gx', 'gy'), may hold values from 0 to 511
- productivity: float32 [64, 8, 256], P('gx', 'gy'), may hold values from 0.3 to 3
Outputs:
- adjoint_early: float32 [2, 20, 512, 1024], P(None, None, 'gx', 'gy')
- well_partials: float32 [4, 512], P(None, 'gx')
Inputs may be any that keep to these rules, and one draw needn't show every extreme that they name: `accumulation`: off-diagonal entries c1, c2 lie within 0.021 in magnitude, diagonal entries c0, c3 from 0.05 to 0.302. `mobility_late`: off-diagonal entries b1, b2 lie within 0.25 in magnitude, diagonal entries b0, b3 from 0.6 to 1.4. `mobility_early`: off-diagonal entries b1, b2 lie within 0.25 in magnitude, diagonal entries b0, b3 from 0.6 to 1.4.
All inputs are finite; a program needn't handle non-finite values.
Results may differ from a plain program's by a relative error of at most 0.0003.
Values may be sent and summed in bfloat16 or wider, within the bound.
A program may use at most 64 MiB of HBM per device.

v0:
```python
import jax
import jax.numpy as jnp
from jax import lax
from jax.sharding import PartitionSpec as P

SWEEPS = 3
WELL_DEV = 8


def shifted(block, axis, distance):
    devices = range(lax.axis_size(axis))
    route = [(i - distance, i) for i in devices if i - distance in devices]
    return lax.ppermute(block, axis, route)


def extended(cells, sides, width):
    for axis, dim in sides:
        count = lax.axis_size(axis)
        ends = count - 1
        head = lax.slice_in_dim(cells, 0, width, axis=dim)
        tail = lax.slice_in_dim(cells, cells.shape[dim] - width, cells.shape[dim], axis=dim)
        cells = jnp.concatenate(
            [
                lax.ppermute(tail, axis, [(i, (i + 1) % count) for i in range(ends)]),
                cells,
                lax.ppermute(head, axis, [((i + 1) % count, i) for i in range(ends)]),
            ],
            axis=dim,
        )
    return cells


def transpose_apply(matrix, vector):
    return jnp.stack(
        [
            matrix[0] * vector[0] + matrix[2] * vector[1],
            matrix[1] * vector[0] + matrix[3] * vector[1],
        ]
    )


def face_total(padded_x, padded_y, layer_trans):
    upper_trans = jnp.concatenate([layer_trans[1:], jnp.zeros_like(layer_trans[:1])], 0)
    return (
        padded_x[:, 1:-1, 1:-1]
        + padded_x[:, 2:, 1:-1]
        + padded_y[:, 1:-1, 1:-1]
        + padded_y[:, 1:-1, 2:]
        + layer_trans
        + upper_trans
    )


def diag_inverse(padded_x, padded_y, layer_trans, accum_full, mobility, inside):
    facesum = face_total(padded_x, padded_y, layer_trans)
    diag_block = accum_full + facesum[None] * mobility
    determinant = diag_block[0] * diag_block[3] - diag_block[1] * diag_block[2]
    determinant = jnp.where(inside > 0, determinant, jnp.float32(1.0))
    det_scale = inside / determinant
    return jnp.stack(
        [
            diag_block[3] * det_scale,
            -diag_block[1] * det_scale,
            -diag_block[2] * det_scale,
            diag_block[0] * det_scale,
        ]
    )


def jacobi_sweep(adjoint_pad, padded_x, padded_y, layer_trans, source, mobility, inverse):
    centre = adjoint_pad[:, :, 1:-1, 1:-1]
    inflow = (
        padded_x[None, :, 1:-1, 1:-1] * adjoint_pad[:, :, :-2, 1:-1]
        + padded_x[None, :, 2:, 1:-1] * adjoint_pad[:, :, 2:, 1:-1]
    )
    inflow = (
        inflow
        + padded_y[None, :, 1:-1, 1:-1] * adjoint_pad[:, :, 1:-1, :-2]
        + padded_y[None, :, 1:-1, 2:] * adjoint_pad[:, :, 1:-1, 2:]
    )
    zero_layer = jnp.zeros_like(centre[:, :1])
    lower_cell = jnp.concatenate([zero_layer, centre[:, :-1]], 1)
    upper_cell = jnp.concatenate([centre[:, 1:], zero_layer], 1)
    upper_trans = jnp.concatenate([layer_trans[1:], jnp.zeros_like(layer_trans[:1])], 0)
    inflow = inflow + layer_trans[None] * lower_cell + upper_trans[None] * upper_cell
    return transpose_apply(inverse, source + transpose_apply(mobility, inflow))


def per_device(
    grad_late,
    grad_early,
    accumulation,
    mobility_late,
    mobility_early,
    trans_x,
    trans_y,
    trans_z,
    perf_cell,
    perf_well,
    productivity,
):
    layers, rows, columns = trans_x.shape
    row_ids = lax.axis_index("gx") * rows + jnp.arange(rows)
    col_ids = lax.axis_index("gy") * columns + jnp.arange(columns)
    layer_ids = jnp.arange(layers)
    masked_x = trans_x.astype(jnp.float32) * (row_ids > 0).astype(jnp.float32)[None, :, None]
    masked_y = trans_y.astype(jnp.float32) * (col_ids > 0).astype(jnp.float32)[None, None, :]
    masked_z = trans_z.astype(jnp.float32) * (layer_ids > 0).astype(jnp.float32)[:, None, None]
    above_x = shifted(masked_x[:, :1, :].astype(jnp.bfloat16), "gx", -1).astype(jnp.float32)
    above_y = shifted(masked_y[:, :, :1].astype(jnp.bfloat16), "gy", -1).astype(jnp.float32)
    padded_x = jnp.concatenate([jnp.zeros_like(above_x), masked_x, above_x], 1)
    padded_x = jnp.pad(padded_x, ((0, 0), (0, 0), (1, 1)))
    padded_y = jnp.concatenate([jnp.zeros_like(above_y), masked_y, above_y], 2)
    padded_y = jnp.pad(padded_y, ((0, 0), (1, 1), (0, 0)))
    inside = jnp.ones((layers, rows, columns), jnp.float32)
    accum_full = accumulation.astype(jnp.float32)

    def solve(source, mobility_arg):
        mobility = mobility_arg.astype(jnp.float32)
        inverse = diag_inverse(padded_x, padded_y, masked_z, accum_full, mobility, inside)
        adjoint = transpose_apply(inverse, source)
        for sweep_index in range(SWEEPS):
            adjoint_pad = extended(adjoint, (("gx", 2), ("gy", 3)), 1)
            adjoint = jacobi_sweep(
                adjoint_pad, padded_x, padded_y, masked_z, source, mobility, inverse
            )
        return adjoint

    adjoint_late = solve(grad_late, mobility_late)
    adjoint_early = solve(grad_early + transpose_apply(accum_full, adjoint_late), mobility_early)
    values = jnp.concatenate([adjoint_early, adjoint_late], 0).reshape(4, -1)
    cell_ids = perf_cell.reshape(-1)
    well_ids = perf_well.reshape(-1)
    picked = jnp.take(values, cell_ids, axis=1) * productivity.reshape(-1)[None]
    nwells = WELL_DEV * lax.axis_size("gx")
    onehot = (well_ids[:, None] == jnp.arange(nwells)[None, :]).astype(jnp.float32)
    partial_value = jnp.dot(
        picked, onehot, precision=lax.Precision.HIGHEST, preferred_element_type=jnp.float32
    )
    owned = lax.psum_scatter(partial_value, "gx", scatter_dimension=1, tiled=True)
    well_partials = lax.psum(owned, "gy")
    return (adjoint_early, well_partials)


def solution(mesh):
    return jax.shard_map(
        per_device,
        mesh=mesh,
        in_specs=(
            P(None, None, "gx", "gy"),
            P(None, None, "gx", "gy"),
            P(None, None, "gx", "gy"),
            P(None, None, "gx", "gy"),
            P(None, None, "gx", "gy"),
            P(None, "gx", "gy"),
            P(None, "gx", "gy"),
            P(None, "gx", "gy"),
            P("gx", "gy", None),
            P("gx", "gy", None),
            P("gx", "gy", None),
        ),
        out_specs=(P(None, None, "gx", "gy"), P(None, "gx")),
        check_vma=False,
    )
```

profile of v0, /device:TPU:128, one launch (start us, length us, event | category | flops | bytes accessed | tf_op | source)
XLA Modules:
  0.0 320.5 jit_solution(5821516998994916361)
XLA Ops:
  0.7 0.9 convert_multiply_fusion.1
  1.6 1.3 collective-permute-start.1
  3.0 2.4 collective-permute-start
  5.4 0.9 convert_multiply_fusion
  6.2 2.8 collective-permute-done.1
  9.1 0.9 add_add_fusion
  10.0 1.2 multiply_add_fusion.1
  11.2 1.0 multiply_add_fusion.29
  12.2 1.0 multiply_add_fusion.28
  13.2 1.9 collective-permute-start.2
  15.2 5.9 %collective-permute-start.3 = (f32[2,20,1,128]{3,2,1,0:T(1,128)S(1)}, f32[2,20,1,128]{3,2,1,0:T(1,128)S(1)}, u32[]{:S(2)}, u32[]{:S(2)}) collective-permute-start(f32[2,20,1,128]{3,2,1,0:T(1,128)S(1)} %get-tuple-element.68), channel_id=1, source_target_pairs={{8,0},{16,8},{24,16},{32,24},{40,32},{48,40},{56,48},{64,56},{72,6... | collective-permute-start | bytes 61448 | tf_op jit(solution)/shard_map/ppermute | solution.py:26
  21.0 0.9 convert_element_type.62
  22.0 0.5 collective-permute-done.3
  22.7 5.8 %collective-permute-start.4 = (f32[2,20,10,1]{3,2,1,0:T(8,128)S(1)}, f32[2,20,10,1]{3,2,1,0:T(8,128)S(1)}, u32[]{:S(2)}, u32[]{:S(2)}) collective-permute-start(f32[2,20,10,1]{3,2,1,0:T(8,128)S(1)} %get-tuple-element.43), channel_id=1, source_target_pairs={{0,1},{1,2},{2,3},{3,4},{4,5},{5,6},{6,7},{8,9},{9,10},{10,11},{11... | collective-permute-start | bytes 4808 | tf_op jit(solution)/shard_map/ppermute | solution.py:24
  28.6 1.3 collective-permute-start.5
  29.9 5.0 %collective-permute-done.4 = f32[2,20,10,1]{3,2,1,0:T(8,128)S(1)} collective-permute-done((f32[2,20,10,1]{3,2,1,0:T(8,128)S(1)}, f32[2,20,10,1]{3,2,1,0:T(8,128)S(1)}, u32[]{:S(2)}, u32[]{:S(2)}) %collective-permute-start.4) | collective-permute-done | bytes 1632 | tf_op jit(solution)/shard_map/ppermute | solution.py:24
  34.9 9.3 %collective-permute-done.5 = f32[2,20,10,1]{3,2,1,0:T(8,128)S(1)} collective-permute-done((f32[2,20,10,1]{3,2,1,0:T(8,128)S(1)}, f32[2,20,10,1]{3,2,1,0:T(8,128)S(1)}, u32[]{:S(2)}, u32[]{:S(2)}) %collective-permute-start.5) | collective-permute-done | bytes 1632 | tf_op jit(solution)/shard_map/ppermute | solution.py:26
  44.5 0.9 maximum_add_fusion
  45.6 1.9 collective-permute-start.6
  47.5 5.8 %collective-permute-start.7 = (f32[2,20,1,128]{3,2,1,0:T(1,128)S(1)}, f32[2,20,1,128]{3,2,1,0:T(1,128)S(1)}, u32[]{:S(2)}, u32[]{:S(2)}) collective-permute-start(f32[2,20,1,128]{3,2,1,0:T(1,128)S(1)} %get-tuple-element.64), channel_id=1, source_target_pairs={{8,0},{16,8},{24,16},{32,24},{40,32},{48,40},{56,48},{64,56},{72,6... | collective-permute-start | bytes 61448 | tf_op jit(solution)/shard_map/ppermute | solution.py:26
  53.3 1.4 collective-permute-done.7
  54.9 4.6 %collective-permute-start.8 = (f32[2,20,10,1]{3,2,1,0:T(8,128)S(1)}, f32[2,20,10,1]{3,2,1,0:T(8,128)S(1)}, u32[]{:S(2)}, u32[]{:S(2)}) collective-permute-start(f32[2,20,10,1]{3,2,1,0:T(8,128)S(1)} %get-tuple-element.41), channel_id=1, source_target_pairs={{0,1},{1,2},{2,3},{3,4},{4,5},{5,6},{6,7},{8,9},{9,10},{10,11},{11... | collective-permute-start | bytes 4808 | tf_op jit(solution)/shard_map/ppermute | solution.py:24
  59.6 1.3 collective-permute-start.9
  60.9 3.2 %collective-permute-done.8 = f32[2,20,10,1]{3,2,1,0:T(8,128)S(1)} collective-permute-done((f32[2,20,10,1]{3,2,1,0:T(8,128)S(1)}, f32[2,20,10,1]{3,2,1,0:T(8,128)S(1)}, u32[]{:S(2)}, u32[]{:S(2)}) %collective-permute-start.8) | collective-permute-done | bytes 1632 | tf_op jit(solution)/shard_map/ppermute | solution.py:24
  64.1 9.3 %collective-permute-done.9 = f32[2,20,10,1]{3,2,1,0:T(8,128)S(1)} collective-permute-done((f32[2,20,10,1]{3,2,1,0:T(8,128)S(1)}, f32[2,20,10,1]{3,2,1,0:T(8,128)S(1)}, u32[]{:S(2)}, u32[]{:S(2)}) %collective-permute-start.9) | collective-permute-done | bytes 1632 | tf_op jit(solution)/shard_map/ppermute | solution.py:26
  73.8 1.9 collective-permute-start.10
  75.8 5.8 %collective-permute-start.11 = (f32[2,20,1,128]{3,2,1,0:T(1,128)S(1)}, f32[2,20,1,128]{3,2,1,0:T(1,128)S(1)}, u32[]{:S(2)}, u32[]{:S(2)}) collective-permute-start(f32[2,20,1,128]{3,2,1,0:T(1,128)S(1)} %get-tuple-element.60), channel_id=1, source_target_pairs={{8,0},{16,8},{24,16},{32,24},{40,32},{48,40},{56,48},{64,56},{72,6... | collective-permute-start | bytes 61448 | tf_op jit(solution)/shard_map/ppermute | solution.py:26
  81.6 1.4 collective-permute-done.11
  83.2 4.5 %collective-permute-start.12 = (f32[2,20,10,1]{3,2,1,0:T(8,128)S(1)}, f32[2,20,10,1]{3,2,1,0:T(8,128)S(1)}, u32[]{:S(2)}, u32[]{:S(2)}) collective-permute-start(f32[2,20,10,1]{3,2,1,0:T(8,128)S(1)} %get-tuple-element.39), channel_id=1, source_target_pairs={{0,1},{1,2},{2,3},{3,4},{4,5},{5,6},{6,7},{8,9},{9,10},{10,11},{11... | collective-permute-start | bytes 4808 | tf_op jit(solution)/shard_map/ppermute | solution.py:24
  87.7 1.3 collective-permute-start.13
  89.0 4.4 %collective-permute-done.12 = f32[2,20,10,1]{3,2,1,0:T(8,128)S(1)} collective-permute-done((f32[2,20,10,1]{3,2,1,0:T(8,128)S(1)}, f32[2,20,10,1]{3,2,1,0:T(8,128)S(1)}, u32[]{:S(2)}, u32[]{:S(2)}) %collective-permute-start.12) | collective-permute-done | bytes 1632 | tf_op jit(solution)/shard_map/ppermute | solution.py:24
  93.4 9.3 %collective-permute-done.13 = f32[2,20,10,1]{3,2,1,0:T(8,128)S(1)} collective-permute-done((f32[2,20,10,1]{3,2,1,0:T(8,128)S(1)}, f32[2,20,10,1]{3,2,1,0:T(8,128)S(1)}, u32[]{:S(2)}, u32[]{:S(2)}) %collective-permute-start.13) | collective-permute-done | bytes 1632 | tf_op jit(solution)/shard_map/ppermute | solution.py:26
  102.8 0.3 fusion.33
  103.4 1.9 collective-permute-start.14
  105.3 5.8 %collective-permute-start.15 = (f32[2,20,1,128]{3,2,1,0:T(1,128)S(1)}, f32[2,20,1,128]{3,2,1,0:T(1,128)S(1)}, u32[]{:S(2)}, u32[]{:S(2)}) collective-permute-start(f32[2,20,1,128]{3,2,1,0:T(1,128)S(1)} %get-tuple-element.58), channel_id=1, source_target_pairs={{8,0},{16,8},{24,16},{32,24},{40,32},{48,40},{56,48},{64,56},{72,6... | collective-permute-start | bytes 61448 | tf_op jit(solution)/shard_map/ppermute | solution.py:26
  111.1 1.4 collective-permute-done.15
  112.7 3.8 %collective-permute-start.16 = (f32[2,20,10,1]{3,2,1,0:T(8,128)S(1)}, f32[2,20,10,1]{3,2,1,0:T(8,128)S(1)}, u32[]{:S(2)}, u32[]{:S(2)}) collective-permute-start(f32[2,20,10,1]{3,2,1,0:T(8,128)S(1)} %get-tuple-element.37), channel_id=1, source_target_pairs={{0,1},{1,2},{2,3},{3,4},{4,5},{5,6},{6,7},{8,9},{9,10},{10,11},{11... | collective-permute-start | bytes 4808 | tf_op jit(solution)/shard_map/ppermute | solution.py:24
  116.6 1.3 collective-permute-start.17
  117.9 4.0 %collective-permute-done.16 = f32[2,20,10,1]{3,2,1,0:T(8,128)S(1)} collective-permute-done((f32[2,20,10,1]{3,2,1,0:T(8,128)S(1)}, f32[2,20,10,1]{3,2,1,0:T(8,128)S(1)}, u32[]{:S(2)}, u32[]{:S(2)}) %collective-permute-start.16) | collective-permute-done | bytes 1632 | tf_op jit(solution)/shard_map/ppermute | solution.py:24
  121.9 7.8 %collective-permute-done.17 = f32[2,20,10,1]{3,2,1,0:T(8,128)S(1)} collective-permute-done((f32[2,20,10,1]{3,2,1,0:T(8,128)S(1)}, f32[2,20,10,1]{3,2,1,0:T(8,128)S(1)}, u32[]{:S(2)}, u32[]{:S(2)}) %collective-permute-start.17) | collective-permute-done | bytes 1632 | tf_op jit(solution)/shard_map/ppermute | solution.py:26
  129.6 0.3 fusion.23
  130.1 1.9 collective-permute-start.18
  132.0 5.8 %collective-permute-start.19 = (f32[2,20,1,128]{3,2,1,0:T(1,128)S(1)}, f32[2,20,1,128]{3,2,1,0:T(1,128)S(1)}, u32[]{:S(2)}, u32[]{:S(2)}) collective-permute-start(f32[2,20,1,128]{3,2,1,0:T(1,128)S(1)} %get-tuple-element.54), channel_id=1, source_target_pairs={{8,0},{16,8},{24,16},{32,24},{40,32},{48,40},{56,48},{64,56},{72,6... | collective-permute-start | bytes 61448 | tf_op jit(solution)/shard_map/ppermute | solution.py:26
  137.8 1.4 collective-permute-done.19
  139.5 1.9 collective-permute-start.20
  141.4 1.3 collective-permute-start.21
  142.7 4.5 %collective-permute-done.20 = f32[2,20,10,1]{3,2,1,0:T(8,128)S(1)} collective-permute-done((f32[2,20,10,1]{3,2,1,0:T(8,128)S(1)}, f32[2,20,10,1]{3,2,1,0:T(8,128)S(1)}, u32[]{:S(2)}, u32[]{:S(2)}) %collective-permute-start.20) | collective-permute-done | bytes 1632 | tf_op jit(solution)/shard_map/ppermute | solution.py:24
  147.2 7.8 %collective-permute-done.21 = f32[2,20,10,1]{3,2,1,0:T(8,128)S(1)} collective-permute-done((f32[2,20,10,1]{3,2,1,0:T(8,128)S(1)}, f32[2,20,10,1]{3,2,1,0:T(8,128)S(1)}, u32[]{:S(2)}, u32[]{:S(2)}) %collective-permute-start.21) | collective-permute-done | bytes 1632 | tf_op jit(solution)/shard_map/ppermute | solution.py:26
  155.0 0.3 fusion.13
  155.4 1.9 collective-permute-start.22
  157.3 5.8 %collective-permute-start.23 = (f32[2,20,1,128]{3,2,1,0:T(1,128)S(1)}, f32[2,20,1,128]{3,2,1,0:T(1,128)S(1)}, u32[]{:S(2)}, u32[]{:S(2)}) collective-permute-start(f32[2,20,1,128]{3,2,1,0:T(1,128)S(1)} %get-tuple-element.50), channel_id=1, source_target_pairs={{8,0},{16,8},{24,16},{32,24},{40,32},{48,40},{56,48},{64,56},{72,6... | collective-permute-start | bytes 61448 | tf_op jit(solution)/shard_map/ppermute | solution.py:26
  163.1 1.3 dynamic-slice
  165.3 1.5 collective-permute-start.24
  166.8 1.3 collective-permute-start.25
  168.1 3.9 %collective-permute-done.24 = f32[2,20,10,1]{3,2,1,0:T(8,128)S(1)} collective-permute-done((f32[2,20,10,1]{3,2,1,0:T(8,128)S(1)}, f32[2,20,10,1]{3,2,1,0:T(8,128)S(1)}, u32[]{:S(2)}, u32[]{:S(2)}) %collective-permute-start.24) | collective-permute-done | bytes 1632 | tf_op jit(solution)/shard_map/ppermute | solution.py:24
  172.0 7.8 %collective-permute-done.25 = f32[2,20,10,1]{3,2,1,0:T(8,128)S(1)} collective-permute-done((f32[2,20,10,1]{3,2,1,0:T(8,128)S(1)}, f32[2,20,10,1]{3,2,1,0:T(8,128)S(1)}, u32[]{:S(2)}, u32[]{:S(2)}) %collective-permute-start.25) | collective-permute-done | bytes 1632 | tf_op jit(solution)/shard_map/ppermute | solution.py:26
  179.7 0.3 fusion.3
  180.1 0.7 pad_maximum_fusion.79
  180.8 0.3 pad_maximum_fusion.6
  181.1 5.5 %copy.17 = f32[4,20480]{0,1:T(8,128)} copy(f32[4,20480]{1,0:T(4,128)S(1)} %pad_maximum_fusion.6) | data formatting | bytes 655360 | tf_op jit(solution)/shard_map/concatenate | solution.py:131
  186.7 4.7 %gather_fusion = f32[256,4]{1,0:T(8,128)S(1)} fusion(f32[4,20480]{0,1:T(8,128)} %copy.17, s32[1024]{0:T(1024)S(1)} %pad_clamp_fusion), kind=kCustom, calls=%fused_computation | custom fusion | bytes 9216 | tf_op jit(solution)/shard_map/jit(_take)/gather | solution.py:134
  191.4 0.4 fusion
  191.8 108.2 %all-reduce.13 = f32[4,512]{1,0:T(4,128)S(1)} all-reduce(f32[4,512]{1,0:T(4,128)S(1)} %fusion), channel_id=2, replica_groups=mesh['gx'=64,'gy'=8] {'gx'}, use_global_device_ids=true, to_apply=%region_0.1.clone | all-reduce | flops 2048 | bytes 16384
  300.0 20.5 %psum.7 = f32[4,8]{1,0:T(4,128)} all-reduce(f32[4,8]{1,0:T(4,128)S(1)} %constant_dynamic-slice_fusion), channel_id=1, replica_groups=mesh['gx'=64,'gy'=8] {'gy'}, use_global_device_ids=true, to_apply=%region_1.2 | all-reduce | flops 32 | bytes 256 | tf_op jit(solution)/shard_map/psum | solution.py:141
  (83 shorter events, 3.1 us)
Async XLA Ops:
  0.6 80.9 %copy-start.2 = (bf16[4,20,8,128]{3,2,1,0:T(8,128)(2,1)S(1)}, bf16[4,20,8,128]{3,2,1,0:T(8,128)(2,1)}, u32[]{:S(2)}) copy-start(bf16[4,20,8,128]{3,2,1,0:T(8,128)(2,1)} %param.13) | copy-start | bytes 491524
  0.6 73.1 %copy-start = (f32[2,20,8,128]{3,2,1,0:T(8,128)S(1)}, f32[2,20,8,128]{3,2,1,0:T(8,128)}, u32[]{:S(2)}) copy-start(f32[2,20,8,128]{3,2,1,0:T(8,128)} %param.11) | copy-start | bytes 491524
  1.6 7.4 %collective-permute-start.1 = (bf16[20,8,1]{2,1,0:T(8,128)(2,1)S(1)}, bf16[20,8,1]{2,1,0:T(8,128)(2,1)S(1)}, u32[]{:S(2)}, u32[]{:S(2)}) collective-permute-start(bf16[20,8,1]{2,1,0:T(8,128)(2,1)S(1)} %slice.794), channel_id=1, source_target_pairs={{1,0},{2,1},{3,2},{4,3},{5,4},{6,5},{7,6},{9,8},{10,9},{11,10},{12... | collective-permute-start | bytes 968 | tf_op jit(solution)/shard_map/ppermute | solution.py:13
  3.0 6.1 %collective-permute-start = (bf16[20,1,128]{2,1,0:T(2,128)(2,1)S(1)}, bf16[20,1,128]{2,1,0:T(2,128)(2,1)S(1)}, u32[]{:S(2)}, u32[]{:S(2)}) collective-permute-start(bf16[20,1,128]{2,1,0:T(2,128)(2,1)S(1)} %slice.795), channel_id=1, source_target_pairs={{8,0},{16,8},{24,16},{32,24},{40,32},{48,40},{56,48},{64,56},{72,6... | collective-permute-start | bytes 15368 | tf_op jit(solution)/shard_map/ppermute | solution.py:13
  11.2 92.0 %copy-start.1 = (f32[2,20,8,128]{3,2,1,0:T(8,128)S(1)}, f32[2,20,8,128]{3,2,1,0:T(8,128)}, u32[]{:S(2)}) copy-start(f32[2,20,8,128]{3,2,1,0:T(8,128)} %param.12) | copy-start | bytes 491524
  13.2 8.8 %collective-permute-start.2 = (f32[2,20,1,128]{3,2,1,0:T(1,128)S(1)}, f32[2,20,1,128]{3,2,1,0:T(1,128)S(1)}, u32[]{:S(2)}, u32[]{:S(2)}) collective-permute-start(f32[2,20,1,128]{3,2,1,0:T(1,128)S(1)} %get-tuple-element.67), channel_id=1, source_target_pairs={{0,8},{8,16},{16,24},{24,32},{32,40},{40,48},{48,56},{56,64},{64,7... | collective-permute-start | bytes 61448 | tf_op jit(solution)/shard_map/ppermute | solution.py:24
  15.1 95.9 %copy-start.4 = (s32[1,1,256]{2,1,0:T(1,128)S(1)}, s32[1,1,256]{2,1,0:T(1,128)}, u32[]{:S(2)}) copy-start(s32[1,1,256]{2,1,0:T(1,128)} %param.19) | copy-start | bytes 3076
  15.1 95.9 %copy-start.3 = (bf16[4,20,8,128]{3,2,1,0:T(8,128)(2,1)S(1)}, bf16[4,20,8,128]{3,2,1,0:T(8,128)(2,1)}, u32[]{:S(2)}) copy-start(bf16[4,20,8,128]{3,2,1,0:T(8,128)(2,1)} %param.15) | copy-start | bytes 491524
  15.2 7.4 %collective-permute-start.3 = (f32[2,20,1,128]{3,2,1,0:T(1,128)S(1)}, f32[2,20,1,128]{3,2,1,0:T(1,128)S(1)}, u32[]{:S(2)}, u32[]{:S(2)}) collective-permute-start(f32[2,20,1,128]{3,2,1,0:T(1,128)S(1)} %get-tuple-element.68), channel_id=1, source_target_pairs={{8,0},{16,8},{24,16},{32,24},{40,32},{48,40},{56,48},{64,56},{72,6... | collective-permute-start | bytes 61448 | tf_op jit(solution)/shard_map/ppermute | solution.py:26
  22.7 12.1 %collective-permute-start.4 = (f32[2,20,10,1]{3,2,1,0:T(8,128)S(1)}, f32[2,20,10,1]{3,2,1,0:T(8,128)S(1)}, u32[]{:S(2)}, u32[]{:S(2)}) collective-permute-start(f32[2,20,10,1]{3,2,1,0:T(8,128)S(1)} %get-tuple-element.43), channel_id=1, source_target_pairs={{0,1},{1,2},{2,3},{3,4},{4,5},{5,6},{6,7},{8,9},{9,10},{10,11},{11... | collective-permute-start | bytes 4808 | tf_op jit(solution)/shard_map/ppermute | solution.py:24
  28.6 15.6 %collective-permute-start.5 = (f32[2,20,10,1]{3,2,1,0:T(8,128)S(1)}, f32[2,20,10,1]{3,2,1,0:T(8,128)S(1)}, u32[]{:S(2)}, u32[]{:S(2)}) collective-permute-start(f32[2,20,10,1]{3,2,1,0:T(8,128)S(1)} %get-tuple-element.44), channel_id=1, source_target_pairs={{1,0},{2,1},{3,2},{4,3},{5,4},{6,5},{7,6},{9,8},{10,9},{11,10},{12... | collective-permute-start | bytes 4808 | tf_op jit(solution)/shard_map/ppermute | solution.py:26
  45.6 7.7 %collective-permute-start.6 = (f32[2,20,1,128]{3,2,1,0:T(1,128)S(1)}, f32[2,20,1,128]{3,2,1,0:T(1,128)S(1)}, u32[]{:S(2)}, u32[]{:S(2)}) collective-permute-start(f32[2,20,1,128]{3,2,1,0:T(1,128)S(1)} %get-tuple-element.63), channel_id=1, source_target_pairs={{0,8},{8,16},{16,24},{24,32},{32,40},{40,48},{48,56},{56,64},{64,7... | collective-permute-start | bytes 61448 | tf_op jit(solution)/shard_map/ppermute | solution.py:24
  47.5 7.2 %collective-permute-start.7 = (f32[2,20,1,128]{3,2,1,0:T(1,128)S(1)}, f32[2,20,1,128]{3,2,1,0:T(1,128)S(1)}, u32[]{:S(2)}, u32[]{:S(2)}) collective-permute-start(f32[2,20,1,128]{3,2,1,0:T(1,128)S(1)} %get-tuple-element.64), channel_id=1, source_target_pairs={{8,0},{16,8},{24,16},{32,24},{40,32},{48,40},{56,48},{64,56},{72,6... | collective-permute-start | bytes 61448 | tf_op jit(solution)/shard_map/ppermute | solution.py:26
  54.9 9.2 %collective-permute-start.8 = (f32[2,20,10,1]{3,2,1,0:T(8,128)S(1)}, f32[2,20,10,1]{3,2,1,0:T(8,128)S(1)}, u32[]{:S(2)}, u32[]{:S(2)}) collective-permute-start(f32[2,20,10,1]{3,2,1,0:T(8,128)S(1)} %get-tuple-element.41), channel_id=1, source_target_pairs={{0,1},{1,2},{2,3},{3,4},{4,5},{5,6},{6,7},{8,9},{9,10},{10,11},{11... | collective-permute-start | bytes 4808 | tf_op jit(solution)/shard_map/ppermute | solution.py:24
  59.6 13.8 %collective-permute-start.9 = (f32[2,20,10,1]{3,2,1,0:T(8,128)S(1)}, f32[2,20,10,1]{3,2,1,0:T(8,128)S(1)}, u32[]{:S(2)}, u32[]{:S(2)}) collective-permute-start(f32[2,20,10,1]{3,2,1,0:T(8,128)S(1)} %get-tuple-element.42), channel_id=1, source_target_pairs={{1,0},{2,1},{3,2},{4,3},{5,4},{6,5},{7,6},{9,8},{10,9},{11,10},{12... | collective-permute-start | bytes 4808 | tf_op jit(solution)/shard_map/ppermute | solution.py:26
  73.8 7.7 %collective-permute-start.10 = (f32[2,20,1,128]{3,2,1,0:T(1,128)S(1)}, f32[2,20,1,128]{3,2,1,0:T(1,128)S(1)}, u32[]{:S(2)}, u32[]{:S(2)}) collective-permute-start(f32[2,20,1,128]{3,2,1,0:T(1,128)S(1)} %get-tuple-element.59), channel_id=1, source_target_pairs={{0,8},{8,16},{16,24},{24,32},{32,40},{40,48},{48,56},{56,64},{64,7... | collective-permute-start | bytes 61448 | tf_op jit(solution)/shard_map/ppermute | solution.py:24
  75.8 7.2 %collective-permute-start.11 = (f32[2,20,1,128]{3,2,1,0:T(1,128)S(1)}, f32[2,20,1,128]{3,2,1,0:T(1,128)S(1)}, u32[]{:S(2)}, u32[]{:S(2)}) collective-permute-start(f32[2,20,1,128]{3,2,1,0:T(1,128)S(1)} %get-tuple-element.60), channel_id=1, source_target_pairs={{8,0},{16,8},{24,16},{32,24},{40,32},{48,40},{56,48},{64,56},{72,6... | collective-permute-start | bytes 61448 | tf_op jit(solution)/shard_map/ppermute | solution.py:26
  83.2 10.2 %collective-permute-start.12 = (f32[2,20,10,1]{3,2,1,0:T(8,128)S(1)}, f32[2,20,10,1]{3,2,1,0:T(8,128)S(1)}, u32[]{:S(2)}, u32[]{:S(2)}) collective-permute-start(f32[2,20,10,1]{3,2,1,0:T(8,128)S(1)} %get-tuple-element.39), channel_id=1, source_target_pairs={{0,1},{1,2},{2,3},{3,4},{4,5},{5,6},{6,7},{8,9},{9,10},{10,11},{11... | collective-permute-start | bytes 4808 | tf_op jit(solution)/shard_map/ppermute | solution.py:24
  87.7 15.0 %collective-permute-start.13 = (f32[2,20,10,1]{3,2,1,0:T(8,128)S(1)}, f32[2,20,10,1]{3,2,1,0:T(8,128)S(1)}, u32[]{:S(2)}, u32[]{:S(2)}) collective-permute-start(f32[2,20,10,1]{3,2,1,0:T(8,128)S(1)} %get-tuple-element.40), channel_id=1, source_target_pairs={{1,0},{2,1},{3,2},{4,3},{5,4},{6,5},{7,6},{9,8},{10,9},{11,10},{12... | collective-permute-start | bytes 4808 | tf_op jit(solution)/shard_map/ppermute | solution.py:26
  103.4 7.8 %collective-permute-start.14 = (f32[2,20,1,128]{3,2,1,0:T(1,128)S(1)}, f32[2,20,1,128]{3,2,1,0:T(1,128)S(1)}, u32[]{:S(2)}, u32[]{:S(2)}) collective-permute-start(f32[2,20,1,128]{3,2,1,0:T(1,128)S(1)} %get-tuple-element.57), channel_id=1, source_target_pairs={{0,8},{8,16},{16,24},{24,32},{32,40},{40,48},{48,56},{56,64},{64,7... | collective-permute-start | bytes 61448 | tf_op jit(solution)/shard_map/ppermute | solution.py:24
  105.3 7.2 %collective-permute-start.15 = (f32[2,20,1,128]{3,2,1,0:T(1,128)S(1)}, f32[2,20,1,128]{3,2,1,0:T(1,128)S(1)}, u32[]{:S(2)}, u32[]{:S(2)}) collective-permute-start(f32[2,20,1,128]{3,2,1,0:T(1,128)S(1)} %get-tuple-element.58), channel_id=1, source_target_pairs={{8,0},{16,8},{24,16},{32,24},{40,32},{48,40},{56,48},{64,56},{72,6... | collective-permute-start | bytes 61448 | tf_op jit(solution)/shard_map/ppermute | solution.py:26
  112.7 9.1 %collective-permute-start.16 = (f32[2,20,10,1]{3,2,1,0:T(8,128)S(1)}, f32[2,20,10,1]{3,2,1,0:T(8,128)S(1)}, u32[]{:S(2)}, u32[]{:S(2)}) collective-permute-start(f32[2,20,10,1]{3,2,1,0:T(8,128)S(1)} %get-tuple-element.37), channel_id=1, source_target_pairs={{0,1},{1,2},{2,3},{3,4},{4,5},{5,6},{6,7},{8,9},{9,10},{10,11},{11... | collective-permute-start | bytes 4808 | tf_op jit(solution)/shard_map/ppermute | solution.py:24
  116.6 13.0 %collective-permute-start.17 = (f32[2,20,10,1]{3,2,1,0:T(8,128)S(1)}, f32[2,20,10,1]{3,2,1,0:T(8,128)S(1)}, u32[]{:S(2)}, u32[]{:S(2)}) collective-permute-start(f32[2,20,10,1]{3,2,1,0:T(8,128)S(1)} %get-tuple-element.38), channel_id=1, source_target_pairs={{1,0},{2,1},{3,2},{4,3},{5,4},{6,5},{7,6},{9,8},{10,9},{11,10},{12... | collective-permute-start | bytes 4808 | tf_op jit(solution)/shard_map/ppermute | solution.py:26
  130.1 7.7 %collective-permute-start.18 = (f32[2,20,1,128]{3,2,1,0:T(1,128)S(1)}, f32[2,20,1,128]{3,2,1,0:T(1,128)S(1)}, u32[]{:S(2)}, u32[]{:S(2)}) collective-permute-start(f32[2,20,1,128]{3,2,1,0:T(1,128)S(1)} %get-tuple-element.53), channel_id=1, source_target_pairs={{0,8},{8,16},{16,24},{24,32},{32,40},{40,48},{48,56},{56,64},{64,7... | collective-permute-start | bytes 61448 | tf_op jit(solution)/shard_map/ppermute | solution.py:24
  132.0 7.2 %collective-permute-start.19 = (f32[2,20,1,128]{3,2,1,0:T(1,128)S(1)}, f32[2,20,1,128]{3,2,1,0:T(1,128)S(1)}, u32[]{:S(2)}, u32[]{:S(2)}) collective-permute-start(f32[2,20,1,128]{3,2,1,0:T(1,128)S(1)} %get-tuple-element.54), channel_id=1, source_target_pairs={{8,0},{16,8},{24,16},{32,24},{40,32},{48,40},{56,48},{64,56},{72,6... | collective-permute-start | bytes 61448 | tf_op jit(solution)/shard_map/ppermute | solution.py:26
  139.5 7.7 %collective-permute-start.20 = (f32[2,20,10,1]{3,2,1,0:T(8,128)S(1)}, f32[2,20,10,1]{3,2,1,0:T(8,128)S(1)}, u32[]{:S(2)}, u32[]{:S(2)}) collective-permute-start(f32[2,20,10,1]{3,2,1,0:T(8,128)S(1)} %get-tuple-element.35), channel_id=1, source_target_pairs={{0,1},{1,2},{2,3},{3,4},{4,5},{5,6},{6,7},{8,9},{9,10},{10,11},{11... | collective-permute-start | bytes 4808 | tf_op jit(solution)/shard_map/ppermute | solution.py:24
  141.4 13.6 %collective-permute-start.21 = (f32[2,20,10,1]{3,2,1,0:T(8,128)S(1)}, f32[2,20,10,1]{3,2,1,0:T(8,128)S(1)}, u32[]{:S(2)}, u32[]{:S(2)}) collective-permute-start(f32[2,20,10,1]{3,2,1,0:T(8,128)S(1)} %get-tuple-element.36), channel_id=1, source_target_pairs={{1,0},{2,1},{3,2},{4,3},{5,4},{6,5},{7,6},{9,8},{10,9},{11,10},{12... | collective-permute-start | bytes 4808 | tf_op jit(solution)/shard_map/ppermute | solution.py:26
  142.7 48.7 %copy-start.5 = (s32[1,1,256]{2,1,0:T(1,128)S(1)}, s32[1,1,256]{2,1,0:T(1,128)}, u32[]{:S(2)}) copy-start(s32[1,1,256]{2,1,0:T(1,128)} %param.20) | copy-start | bytes 3076
  142.7 48.7 %copy-start.6 = (f32[1,1,256]{2,1,0:T(1,128)S(1)}, f32[1,1,256]{2,1,0:T(1,128)}, u32[]{:S(2)}) copy-start(f32[1,1,256]{2,1,0:T(1,128)} %param.21) | copy-start | bytes 3076
  155.4 9.6 %collective-permute-start.22 = (f32[2,20,1,128]{3,2,1,0:T(1,128)S(1)}, f32[2,20,1,128]{3,2,1,0:T(1,128)S(1)}, u32[]{:S(2)}, u32[]{:S(2)}) collective-permute-start(f32[2,20,1,128]{3,2,1,0:T(1,128)S(1)} %get-tuple-element.49), channel_id=1, source_target_pairs={{0,8},{8,16},{16,24},{24,32},{32,40},{40,48},{48,56},{56,64},{64,7... | collective-permute-start | bytes 61448 | tf_op jit(solution)/shard_map/ppermute | solution.py:24
  157.3 7.7 %collective-permute-start.23 = (f32[2,20,1,128]{3,2,1,0:T(1,128)S(1)}, f32[2,20,1,128]{3,2,1,0:T(1,128)S(1)}, u32[]{:S(2)}, u32[]{:S(2)}) collective-permute-start(f32[2,20,1,128]{3,2,1,0:T(1,128)S(1)} %get-tuple-element.50), channel_id=1, source_target_pairs={{8,0},{16,8},{24,16},{32,24},{40,32},{48,40},{56,48},{64,56},{72,6... | collective-permute-start | bytes 61448 | tf_op jit(solution)/shard_map/ppermute | solution.py:26
  165.3 6.7 %collective-permute-start.24 = (f32[2,20,10,1]{3,2,1,0:T(8,128)S(1)}, f32[2,20,10,1]{3,2,1,0:T(8,128)S(1)}, u32[]{:S(2)}, u32[]{:S(2)}) collective-permute-start(f32[2,20,10,1]{3,2,1,0:T(8,128)S(1)} %get-tuple-element.33), channel_id=1, source_target_pairs={{0,1},{1,2},{2,3},{3,4},{4,5},{5,6},{6,7},{8,9},{9,10},{10,11},{11... | collective-permute-start | bytes 4808 | tf_op jit(solution)/shard_map/ppermute | solution.py:24
  166.8 13.0 %collective-permute-start.25 = (f32[2,20,10,1]{3,2,1,0:T(8,128)S(1)}, f32[2,20,10,1]{3,2,1,0:T(8,128)S(1)}, u32[]{:S(2)}, u32[]{:S(2)}) collective-permute-start(f32[2,20,10,1]{3,2,1,0:T(8,128)S(1)} %get-tuple-element.34), channel_id=1, source_target_pairs={{1,0},{2,1},{3,2},{4,3},{5,4},{6,5},{7,6},{9,8},{10,9},{11,10},{12... | collective-permute-start | bytes 4808 | tf_op jit(solution)/shard_map/ppermute | solution.py:26
where the time goes:
time: 322 us; the launch traced here: 321 us
  blocking collectives  129 us (40%)
  waiting for transfers between devices  85.2 us (26%)
  starting transfers between devices  79.7 us (25%)
  local copies, waits for them, and re-layouts  12.6 us (4%)
  other arithmetic  11.9 us (4%)
    unnamed x1, blocking collectives  108 us
    ppermute x12, waiting for transfers between devices, extended(): lax.ppermute(head, axis, [((i + 1) % count, i) for i in range(ends)])  57.5 us
    ppermute x12, starting transfers between devices, extended(): lax.ppermute(head, axis, [((i + 1) % count, i) for i in range(ends)])  42.4 us
    ppermute x12, starting transfers between devices, extended(): lax.ppermute(tail, axis, [(i, (i + 1) % count) for i in range(ends)])  33.6 us
    ppermute x12, waiting for transfers between devices, extended(): lax.ppermute(tail, axis, [(i, (i + 1) % count) for i in range(ends)])  24.9 us
    psum x1, blocking collectives, per_device(): well_partials = lax.psum(owned, 'gy')  20.5 us
  transfers between devices with their start and end apart: 26, of which 18 were waited for; matrix products, arithmetic and copies ran while one was open for 1% of the time, Pallas kernels for 0%

commit v1 on v0

--- a/solution.py
+++ b/solution.py
@@ -1,3 +1,4 @@
+import functools
 import jax
 import jax.numpy as jnp
 from jax import lax
@@ -5,6 +6,13 @@
 
 SWEEPS = 3
 WELL_DEV = 8
+
+
+def follow_the_levels_all(mine_x, peer_axis):
+    return lax.all_gather(mine_x, peer_axis).sum(axis=0)
+
+
+watch_run_on = functools.partial(follow_the_levels_all, peer_axis="gy")
 
 
 def shifted(block, axis, distance):
@@ -138,7 +146,7 @@
         picked, onehot, precision=lax.Precision.HIGHEST, preferred_element_type=jnp.float32
     )
     owned = lax.psum_scatter(partial_value, "gx", scatter_dimension=1, tiled=True)
-    well_partials = lax.psum(owned, "gy")
+    well_partials = watch_run_on(owned)
     return (adjoint_early, well_partials)
 
 

time: 322 us -> 332 us (1.031)
  blocking collectives: 129 us -> 139 us
    all_gather x0 -> x1, blocking collectives: none -> 30.6 us  [follow_the_levels_all(): return lax.all_gather(mine_x, peer_axis).sum(axis=0)]
    psum x1 -> x0, blocking collectives: 20.5 us -> none  [per_device(): well_partials = lax.psum(owned, 'gy')]
where the time goes in v1:
time: 332 us; the launch traced here: 331 us
  blocking collectives  139 us (42%)
  waiting for transfers between devices  85.2 us (26%)
  starting transfers between devices  79.7 us (24%)
  local copies, waits for them, and re-layouts  12.6 us (4%)
  other arithmetic  12.5 us (4%)
    unnamed x1, blocking collectives  108 us
    ppermute x12, waiting for transfers between devices, extended(): lax.ppermute(head, axis, [((i + 1) % count, i) for i in range(ends)])  57.5 us
    ppermute x12, starting transfers between devices, extended(): lax.ppermute(head, axis, [((i + 1) % count, i) for i in range(ends)])  42.4 us
    ppermute x12, starting transfers between devices, extended(): lax.ppermute(tail, axis, [(i, (i + 1) % count) for i in range(ends)])  33.6 us
    all_gather x1, blocking collectives, follow_the_levels_all(): return lax.all_gather(mine_x, peer_axis).sum(axis=0)  30.6 us
    ppermute x12, waiting for transfers between devices, extended(): lax.ppermute(tail, axis, [(i, (i + 1) % count) for i in range(ends)])  24.9 us
  transfers between devices with their start and end apart: 26, of which 18 were waited for; matrix products, arithmetic and copies ran while one was open for 1% of the time, Pallas kernels for 0%

profile of v1, /device:TPU:128, one launch (start us, length us, event | category | flops | bytes accessed | tf_op | source)
XLA Modules:
  0.0 331.2 jit_solution(18151090187962651070)
XLA Ops:
  0.7 0.9 convert_multiply_fusion.1
  1.6 1.3 collective-permute-start.1
  3.0 2.4 collective-permute-start
  5.4 0.9 convert_multiply_fusion
  6.2 2.8 collective-permute-done.1
  9.1 0.9 add_add_fusion
  10.0 1.2 multiply_add_fusion.1
  11.2 1.0 multiply_add_fusion.29
  12.2 1.0 multiply_add_fusion.28
  13.2 1.9 collective-permute-start.2
  15.2 5.9 %collective-permute-start.3 = (f32[2,20,1,128]{3,2,1,0:T(1,128)S(1)}, f32[2,20,1,128]{3,2,1,0:T(1,128)S(1)}, u32[]{:S(2)}, u32[]{:S(2)}) collective-permute-start(f32[2,20,1,128]{3,2,1,0:T(1,128)S(1)} %get-tuple-element.68), channel_id=1, source_target_pairs={{8,0},{16,8},{24,16},{32,24},{40,32},{48,40},{56,48},{64,56},{72,6... | collective-permute-start | bytes 61448 | tf_op jit(solution)/shard_map/ppermute | solution.py:34
  21.0 0.9 convert_element_type.62
  22.0 0.5 collective-permute-done.3
  22.7 5.8 %collective-permute-start.4 = (f32[2,20,10,1]{3,2,1,0:T(8,128)S(1)}, f32[2,20,10,1]{3,2,1,0:T(8,128)S(1)}, u32[]{:S(2)}, u32[]{:S(2)}) collective-permute-start(f32[2,20,10,1]{3,2,1,0:T(8,128)S(1)} %get-tuple-element.43), channel_id=1, source_target_pairs={{0,1},{1,2},{2,3},{3,4},{4,5},{5,6},{6,7},{8,9},{9,10},{10,11},{11... | collective-permute-start | bytes 4808 | tf_op jit(solution)/shard_map/ppermute | solution.py:32
  28.6 1.3 collective-permute-start.5
  29.9 5.0 %collective-permute-done.4 = f32[2,20,10,1]{3,2,1,0:T(8,128)S(1)} collective-permute-done((f32[2,20,10,1]{3,2,1,0:T(8,128)S(1)}, f32[2,20,10,1]{3,2,1,0:T(8,128)S(1)}, u32[]{:S(2)}, u32[]{:S(2)}) %collective-permute-start.4) | collective-permute-done | bytes 1632 | tf_op jit(solution)/shard_map/ppermute | solution.py:32
  34.9 9.3 %collective-permute-done.5 = f32[2,20,10,1]{3,2,1,0:T(8,128)S(1)} collective-permute-done((f32[2,20,10,1]{3,2,1,0:T(8,128)S(1)}, f32[2,20,10,1]{3,2,1,0:T(8,128)S(1)}, u32[]{:S(2)}, u32[]{:S(2)}) %collective-permute-start.5) | collective-permute-done | bytes 1632 | tf_op jit(solution)/shard_map/ppermute | solution.py:34
  44.5 0.9 maximum_add_fusion
  45.6 1.9 collective-permute-start.6
  47.5 5.8 %collective-permute-start.7 = (f32[2,20,1,128]{3,2,1,0:T(1,128)S(1)}, f32[2,20,1,128]{3,2,1,0:T(1,128)S(1)}, u32[]{:S(2)}, u32[]{:S(2)}) collective-permute-start(f32[2,20,1,128]{3,2,1,0:T(1,128)S(1)} %get-tuple-element.64), channel_id=1, source_target_pairs={{8,0},{16,8},{24,16},{32,24},{40,32},{48,40},{56,48},{64,56},{72,6... | collective-permute-start | bytes 61448 | tf_op jit(solution)/shard_map/ppermute | solution.py:34
  53.3 1.4 collective-permute-done.7
  54.9 4.6 %collective-permute-start.8 = (f32[2,20,10,1]{3,2,1,0:T(8,128)S(1)}, f32[2,20,10,1]{3,2,1,0:T(8,128)S(1)}, u32[]{:S(2)}, u32[]{:S(2)}) collective-permute-start(f32[2,20,10,1]{3,2,1,0:T(8,128)S(1)} %get-tuple-element.41), channel_id=1, source_target_pairs={{0,1},{1,2},{2,3},{3,4},{4,5},{5,6},{6,7},{8,9},{9,10},{10,11},{11... | collective-permute-start | bytes 4808 | tf_op jit(solution)/shard_map/ppermute | solution.py:32
  59.6 1.3 collective-permute-start.9
  60.9 3.2 collective-permute-done.8
  64.1 9.3 %collective-permute-done.9 = f32[2,20,10,1]{3,2,1,0:T(8,128)S(1)} collective-permute-done((f32[2,20,10,1]{3,2,1,0:T(8,128)S(1)}, f32[2,20,10,1]{3,2,1,0:T(8,128)S(1)}, u32[]{:S(2)}, u32[]{:S(2)}) %collective-permute-start.9) | collective-permute-done | bytes 1632 | tf_op jit(solution)/shard_map/ppermute | solution.py:34
  73.8 1.9 collective-permute-start.10
  75.8 5.8 %collective-permute-start.11 = (f32[2,20,1,128]{3,2,1,0:T(1,128)S(1)}, f32[2,20,1,128]{3,2,1,0:T(1,128)S(1)}, u32[]{:S(2)}, u32[]{:S(2)}) collective-permute-start(f32[2,20,1,128]{3,2,1,0:T(1,128)S(1)} %get-tuple-element.60), channel_id=1, source_target_pairs={{8,0},{16,8},{24,16},{32,24},{40,32},{48,40},{56,48},{64,56},{72,6... | collective-permute-start | bytes 61448 | tf_op jit(solution)/shard_map/ppermute | solution.py:34
  81.6 1.4 collective-permute-done.11
  83.2 4.5 %collective-permute-start.12 = (f32[2,20,10,1]{3,2,1,0:T(8,128)S(1)}, f32[2,20,10,1]{3,2,1,0:T(8,128)S(1)}, u32[]{:S(2)}, u32[]{:S(2)}) collective-permute-start(f32[2,20,10,1]{3,2,1,0:T(8,128)S(1)} %get-tuple-element.39), channel_id=1, source_target_pairs={{0,1},{1,2},{2,3},{3,4},{4,5},{5,6},{6,7},{8,9},{9,10},{10,11},{11... | collective-permute-start | bytes 4808 | tf_op jit(solution)/shard_map/ppermute | solution.py:32
  87.7 1.3 collective-permute-start.13
  89.0 4.4 %collective-permute-done.12 = f32[2,20,10,1]{3,2,1,0:T(8,128)S(1)} collective-permute-done((f32[2,20,10,1]{3,2,1,0:T(8,128)S(1)}, f32[2,20,10,1]{3,2,1,0:T(8,128)S(1)}, u32[]{:S(2)}, u32[]{:S(2)}) %collective-permute-start.12) | collective-permute-done | bytes 1632 | tf_op jit(solution)/shard_map/ppermute | solution.py:32
  93.4 9.3 %collective-permute-done.13 = f32[2,20,10,1]{3,2,1,0:T(8,128)S(1)} collective-permute-done((f32[2,20,10,1]{3,2,1,0:T(8,128)S(1)}, f32[2,20,10,1]{3,2,1,0:T(8,128)S(1)}, u32[]{:S(2)}, u32[]{:S(2)}) %collective-permute-start.13) | collective-permute-done | bytes 1632 | tf_op jit(solution)/shard_map/ppermute | solution.py:34
  102.8 0.3 fusion.33
  103.4 1.9 collective-permute-start.14
  105.3 5.8 %collective-permute-start.15 = (f32[2,20,1,128]{3,2,1,0:T(1,128)S(1)}, f32[2,20,1,128]{3,2,1,0:T(1,128)S(1)}, u32[]{:S(2)}, u32[]{:S(2)}) collective-permute-start(f32[2,20,1,128]{3,2,1,0:T(1,128)S(1)} %get-tuple-element.58), channel_id=1, source_target_pairs={{8,0},{16,8},{24,16},{32,24},{40,32},{48,40},{56,48},{64,56},{72,6... | collective-permute-start | bytes 61448 | tf_op jit(solution)/shard_map/ppermute | solution.py:34
  111.1 1.4 collective-permute-done.15
  112.7 3.8 %collective-permute-start.16 = (f32[2,20,10,1]{3,2,1,0:T(8,128)S(1)}, f32[2,20,10,1]{3,2,1,0:T(8,128)S(1)}, u32[]{:S(2)}, u32[]{:S(2)}) collective-permute-start(f32[2,20,10,1]{3,2,1,0:T(8,128)S(1)} %get-tuple-element.37), channel_id=1, source_target_pairs={{0,1},{1,2},{2,3},{3,4},{4,5},{5,6},{6,7},{8,9},{9,10},{10,11},{11... | collective-permute-start | bytes 4808 | tf_op jit(solution)/shard_map/ppermute | solution.py:32
  116.6 1.3 collective-permute-start.17
  117.9 4.0 %collective-permute-done.16 = f32[2,20,10,1]{3,2,1,0:T(8,128)S(1)} collective-permute-done((f32[2,20,10,1]{3,2,1,0:T(8,128)S(1)}, f32[2,20,10,1]{3,2,1,0:T(8,128)S(1)}, u32[]{:S(2)}, u32[]{:S(2)}) %collective-permute-start.16) | collective-permute-done | bytes 1632 | tf_op jit(solution)/shard_map/ppermute | solution.py:32
  121.9 7.8 %collective-permute-done.17 = f32[2,20,10,1]{3,2,1,0:T(8,128)S(1)} collective-permute-done((f32[2,20,10,1]{3,2,1,0:T(8,128)S(1)}, f32[2,20,10,1]{3,2,1,0:T(8,128)S(1)}, u32[]{:S(2)}, u32[]{:S(2)}) %collective-permute-start.17) | collective-permute-done | bytes 1632 | tf_op jit(solution)/shard_map/ppermute | solution.py:34
  129.6 0.3 fusion.23
  130.1 1.9 collective-permute-start.18
  132.0 5.8 %collective-permute-start.19 = (f32[2,20,1,128]{3,2,1,0:T(1,128)S(1)}, f32[2,20,1,128]{3,2,1,0:T(1,128)S(1)}, u32[]{:S(2)}, u32[]{:S(2)}) collective-permute-start(f32[2,20,1,128]{3,2,1,0:T(1,128)S(1)} %get-tuple-element.54), channel_id=1, source_target_pairs={{8,0},{16,8},{24,16},{32,24},{40,32},{48,40},{56,48},{64,56},{72,6... | collective-permute-start | bytes 61448 | tf_op jit(solution)/shard_map/ppermute | solution.py:34
  137.8 1.4 collective-permute-done.19
  139.5 1.9 collective-permute-start.20
  141.4 1.3 collective-permute-start.21
  142.7 4.5 %collective-permute-done.20 = f32[2,20,10,1]{3,2,1,0:T(8,128)S(1)} collective-permute-done((f32[2,20,10,1]{3,2,1,0:T(8,128)S(1)}, f32[2,20,10,1]{3,2,1,0:T(8,128)S(1)}, u32[]{:S(2)}, u32[]{:S(2)}) %collective-permute-start.20) | collective-permute-done | bytes 1632 | tf_op jit(solution)/shard_map/ppermute | solution.py:32
  147.2 7.8 %collective-permute-done.21 = f32[2,20,10,1]{3,2,1,0:T(8,128)S(1)} collective-permute-done((f32[2,20,10,1]{3,2,1,0:T(8,128)S(1)}, f32[2,20,10,1]{3,2,1,0:T(8,128)S(1)}, u32[]{:S(2)}, u32[]{:S(2)}) %collective-permute-start.21) | collective-permute-done | bytes 1632 | tf_op jit(solution)/shard_map/ppermute | solution.py:34
  155.0 0.3 fusion.13
  155.4 1.9 collective-permute-start.22
  157.3 5.8 %collective-permute-start.23 = (f32[2,20,1,128]{3,2,1,0:T(1,128)S(1)}, f32[2,20,1,128]{3,2,1,0:T(1,128)S(1)}, u32[]{:S(2)}, u32[]{:S(2)}) collective-permute-start(f32[2,20,1,128]{3,2,1,0:T(1,128)S(1)} %get-tuple-element.50), channel_id=1, source_target_pairs={{8,0},{16,8},{24,16},{32,24},{40,32},{48,40},{56,48},{64,56},{72,6... | collective-permute-start | bytes 61448 | tf_op jit(solution)/shard_map/ppermute | solution.py:34
  163.1 1.3 dynamic-slice
  165.3 1.5 collective-permute-start.24
  166.8 1.3 collective-permute-start.25
  168.1 3.9 %collective-permute-done.24 = f32[2,20,10,1]{3,2,1,0:T(8,128)S(1)} collective-permute-done((f32[2,20,10,1]{3,2,1,0:T(8,128)S(1)}, f32[2,20,10,1]{3,2,1,0:T(8,128)S(1)}, u32[]{:S(2)}, u32[]{:S(2)}) %collective-permute-start.24) | collective-permute-done | bytes 1632 | tf_op jit(solution)/shard_map/ppermute | solution.py:32
  172.0 7.8 %collective-permute-done.25 = f32[2,20,10,1]{3,2,1,0:T(8,128)S(1)} collective-permute-done((f32[2,20,10,1]{3,2,1,0:T(8,128)S(1)}, f32[2,20,10,1]{3,2,1,0:T(8,128)S(1)}, u32[]{:S(2)}, u32[]{:S(2)}) %collective-permute-start.25) | collective-permute-done | bytes 1632 | tf_op jit(solution)/shard_map/ppermute | solution.py:34
  180.1 0.7 pad_maximum_fusion.79
  180.8 0.3 pad_maximum_fusion.6
  181.1 5.5 %copy.17 = f32[4,20480]{0,1:T(8,128)} copy(f32[4,20480]{1,0:T(4,128)S(1)} %pad_maximum_fusion.6) | data formatting | bytes 655360 | tf_op jit(solution)/shard_map/concatenate | solution.py:139
  186.7 4.7 %gather_fusion = f32[256,4]{1,0:T(8,128)S(1)} fusion(f32[4,20480]{0,1:T(8,128)} %copy.17, s32[1024]{0:T(1024)S(1)} %pad_clamp_fusion), kind=kCustom, calls=%fused_computation | custom fusion | bytes 9216 | tf_op jit(solution)/shard_map/jit(_take)/gather | solution.py:142
  191.4 0.4 fusion
  191.8 108.2 %all-reduce.13 = f32[4,512]{1,0:T(4,128)S(1)} all-reduce(f32[4,512]{1,0:T(4,128)S(1)} %fusion), channel_id=3, replica_groups=mesh['gx'=64,'gy'=8] {'gx'}, use_global_device_ids=true, to_apply=%region_0.1.clone | all-reduce | flops 2048 | bytes 16384
  300.0 30.6 %all-gather.1 = f32[8,4,8]{2,1,0:T(4,128)S(1)} all-gather(f32[1,4,8]{2,1,0:T(4,128)S(1)} %dynamic-slice_bitcast_fusion), channel_id=2, replica_groups=mesh['gx'=64,'gy'=8] {'gy'}, dimensions={0}, use_global_device_ids=true | all-gather | bytes 1152 | tf_op jit(solution)/shard_map/all_gather | solution.py:12
  330.6 0.6 reduce_sum.9
  (84 shorter events, 3.4 us)
Async XLA Ops:
  0.6 80.9 %copy-start.2 = (bf16[4,20,8,128]{3,2,1,0:T(8,128)(2,1)S(1)}, bf16[4,20,8,128]{3,2,1,0:T(8,128)(2,1)}, u32[]{:S(2)}) copy-start(bf16[4,20,8,128]{3,2,1,0:T(8,128)(2,1)} %param.13) | copy-start | bytes 491524
  0.6 73.1 %copy-start = (f32[2,20,8,128]{3,2,1,0:T(8,128)S(1)}, f32[2,20,8,128]{3,2,1,0:T(8,128)}, u32[]{:S(2)}) copy-start(f32[2,20,8,128]{3,2,1,0:T(8,128)} %param.11) | copy-start | bytes 491524
  1.6 7.4 %collective-permute-start.1 = (bf16[20,8,1]{2,1,0:T(8,128)(2,1)S(1)}, bf16[20,8,1]{2,1,0:T(8,128)(2,1)S(1)}, u32[]{:S(2)}, u32[]{:S(2)}) collective-permute-start(bf16[20,8,1]{2,1,0:T(8,128)(2,1)S(1)} %slice.794), channel_id=1, source_target_pairs={{1,0},{2,1},{3,2},{4,3},{5,4},{6,5},{7,6},{9,8},{10,9},{11,10},{12... | collective-permute-start | bytes 968 | tf_op jit(solution)/shard_map/ppermute | solution.py:21
  3.0 6.1 %collective-permute-start = (bf16[20,1,128]{2,1,0:T(2,128)(2,1)S(1)}, bf16[20,1,128]{2,1,0:T(2,128)(2,1)S(1)}, u32[]{:S(2)}, u32[]{:S(2)}) collective-permute-start(bf16[20,1,128]{2,1,0:T(2,128)(2,1)S(1)} %slice.795), channel_id=1, source_target_pairs={{8,0},{16,8},{24,16},{32,24},{40,32},{48,40},{56,48},{64,56},{72,6... | collective-permute-start | bytes 15368 | tf_op jit(solution)/shard_map/ppermute | solution.py:21
  11.2 92.0 %copy-start.1 = (f32[2,20,8,128]{3,2,1,0:T(8,128)S(1)}, f32[2,20,8,128]{3,2,1,0:T(8,128)}, u32[]{:S(2)}) copy-start(f32[2,20,8,128]{3,2,1,0:T(8,128)} %param.12) | copy-start | bytes 491524
  13.2 8.8 %collective-permute-start.2 = (f32[2,20,1,128]{3,2,1,0:T(1,128)S(1)}, f32[2,20,1,128]{3,2,1,0:T(1,128)S(1)}, u32[]{:S(2)}, u32[]{:S(2)}) collective-permute-start(f32[2,20,1,128]{3,2,1,0:T(1,128)S(1)} %get-tuple-element.67), channel_id=1, source_target_pairs={{0,8},{8,16},{16,24},{24,32},{32,40},{40,48},{48,56},{56,64},{64,7... | collective-permute-start | bytes 61448 | tf_op jit(solution)/shard_map/ppermute | solution.py:32
  15.1 95.9 %copy-start.4 = (s32[1,1,256]{2,1,0:T(1,128)S(1)}, s32[1,1,256]{2,1,0:T(1,128)}, u32[]{:S(2)}) copy-start(s32[1,1,256]{2,1,0:T(1,128)} %param.19) | copy-start | bytes 3076
  15.1 95.9 %copy-start.3 = (bf16[4,20,8,128]{3,2,1,0:T(8,128)(2,1)S(1)}, bf16[4,20,8,128]{3,2,1,0:T(8,128)(2,1)}, u32[]{:S(2)}) copy-start(bf16[4,20,8,128]{3,2,1,0:T(8,128)(2,1)} %param.15) | copy-start | bytes 491524
  15.2 7.4 %collective-permute-start.3 = (f32[2,20,1,128]{3,2,1,0:T(1,128)S(1)}, f32[2,20,1,128]{3,2,1,0:T(1,128)S(1)}, u32[]{:S(2)}, u32[]{:S(2)}) collective-permute-start(f32[2,20,1,128]{3,2,1,0:T(1,128)S(1)} %get-tuple-element.68), channel_id=1, source_target_pairs={{8,0},{16,8},{24,16},{32,24},{40,32},{48,40},{56,48},{64,56},{72,6... | collective-permute-start | bytes 61448 | tf_op jit(solution)/shard_map/ppermute | solution.py:34
  22.7 12.1 %collective-permute-start.4 = (f32[2,20,10,1]{3,2,1,0:T(8,128)S(1)}, f32[2,20,10,1]{3,2,1,0:T(8,128)S(1)}, u32[]{:S(2)}, u32[]{:S(2)}) collective-permute-start(f32[2,20,10,1]{3,2,1,0:T(8,128)S(1)} %get-tuple-element.43), channel_id=1, source_target_pairs={{0,1},{1,2},{2,3},{3,4},{4,5},{5,6},{6,7},{8,9},{9,10},{10,11},{11... | collective-permute-start | bytes 4808 | tf_op jit(solution)/shard_map/ppermute | solution.py:32
  28.6 15.6 %collective-permute-start.5 = (f32[2,20,10,1]{3,2,1,0:T(8,128)S(1)}, f32[2,20,10,1]{3,2,1,0:T(8,128)S(1)}, u32[]{:S(2)}, u32[]{:S(2)}) collective-permute-start(f32[2,20,10,1]{3,2,1,0:T(8,128)S(1)} %get-tuple-element.44), channel_id=1, source_target_pairs={{1,0},{2,1},{3,2},{4,3},{5,4},{6,5},{7,6},{9,8},{10,9},{11,10},{12... | collective-permute-start | bytes 4808 | tf_op jit(solution)/shard_map/ppermute | solution.py:34
  45.6 7.7 %collective-permute-start.6 = (f32[2,20,1,128]{3,2,1,0:T(1,128)S(1)}, f32[2,20,1,128]{3,2,1,0:T(1,128)S(1)}, u32[]{:S(2)}, u32[]{:S(2)}) collective-permute-start(f32[2,20,1,128]{3,2,1,0:T(1,128)S(1)} %get-tuple-element.63), channel_id=1, source_target_pairs={{0,8},{8,16},{16,24},{24,32},{32,40},{40,48},{48,56},{56,64},{64,7... | collective-permute-start | bytes 61448 | tf_op jit(solution)/shard_map/ppermute | solution.py:32
  47.5 7.2 %collective-permute-start.7 = (f32[2,20,1,128]{3,2,1,0:T(1,128)S(1)}, f32[2,20,1,128]{3,2,1,0:T(1,128)S(1)}, u32[]{:S(2)}, u32[]{:S(2)}) collective-permute-start(f32[2,20,1,128]{3,2,1,0:T(1,128)S(1)} %get-tuple-element.64), channel_id=1, source_target_pairs={{8,0},{16,8},{24,16},{32,24},{40,32},{48,40},{56,48},{64,56},{72,6... | collective-permute-start | bytes 61448 | tf_op jit(solution)/shard_map/ppermute | solution.py:34
  54.9 9.2 %collective-permute-start.8 = (f32[2,20,10,1]{3,2,1,0:T(8,128)S(1)}, f32[2,20,10,1]{3,2,1,0:T(8,128)S(1)}, u32[]{:S(2)}, u32[]{:S(2)}) collective-permute-start(f32[2,20,10,1]{3,2,1,0:T(8,128)S(1)} %get-tuple-element.41), channel_id=1, source_target_pairs={{0,1},{1,2},{2,3},{3,4},{4,5},{5,6},{6,7},{8,9},{9,10},{10,11},{11... | collective-permute-start | bytes 4808 | tf_op jit(solution)/shard_map/ppermute | solution.py:32
  59.6 13.8 %collective-permute-start.9 = (f32[2,20,10,1]{3,2,1,0:T(8,128)S(1)}, f32[2,20,10,1]{3,2,1,0:T(8,128)S(1)}, u32[]{:S(2)}, u32[]{:S(2)}) collective-permute-start(f32[2,20,10,1]{3,2,1,0:T(8,128)S(1)} %get-tuple-element.42), channel_id=1, source_target_pairs={{1,0},{2,1},{3,2},{4,3},{5,4},{6,5},{7,6},{9,8},{10,9},{11,10},{12... | collective-permute-start | bytes 4808 | tf_op jit(solution)/shard_map/ppermute | solution.py:34
  73.8 7.7 %collective-permute-start.10 = (f32[2,20,1,128]{3,2,1,0:T(1,128)S(1)}, f32[2,20,1,128]{3,2,1,0:T(1,128)S(1)}, u32[]{:S(2)}, u32[]{:S(2)}) collective-permute-start(f32[2,20,1,128]{3,2,1,0:T(1,128)S(1)} %get-tuple-element.59), channel_id=1, source_target_pairs={{0,8},{8,16},{16,24},{24,32},{32,40},{40,48},{48,56},{56,64},{64,7... | collective-permute-start | bytes 61448 | tf_op jit(solution)/shard_map/ppermute | solution.py:32
  75.8 7.2 %collective-permute-start.11 = (f32[2,20,1,128]{3,2,1,0:T(1,128)S(1)}, f32[2,20,1,128]{3,2,1,0:T(1,128)S(1)}, u32[]{:S(2)}, u32[]{:S(2)}) collective-permute-start(f32[2,20,1,128]{3,2,1,0:T(1,128)S(1)} %get-tuple-element.60), channel_id=1, source_target_pairs={{8,0},{16,8},{24,16},{32,24},{40,32},{48,40},{56,48},{64,56},{72,6... | collective-permute-start | bytes 61448 | tf_op jit(solution)/shard_map/ppermute | solution.py:34
  83.2 10.2 %collective-permute-start.12 = (f32[2,20,10,1]{3,2,1,0:T(8,128)S(1)}, f32[2,20,10,1]{3,2,1,0:T(8,128)S(1)}, u32[]{:S(2)}, u32[]{:S(2)}) collective-permute-start(f32[2,20,10,1]{3,2,1,0:T(8,128)S(1)} %get-tuple-element.39), channel_id=1, source_target_pairs={{0,1},{1,2},{2,3},{3,4},{4,5},{5,6},{6,7},{8,9},{9,10},{10,11},{11... | collective-permute-start | bytes 4808 | tf_op jit(solution)/shard_map/ppermute | solution.py:32
  87.7 15.0 %collective-permute-start.13 = (f32[2,20,10,1]{3,2,1,0:T(8,128)S(1)}, f32[2,20,10,1]{3,2,1,0:T(8,128)S(1)}, u32[]{:S(2)}, u32[]{:S(2)}) collective-permute-start(f32[2,20,10,1]{3,2,1,0:T(8,128)S(1)} %get-tuple-element.40), channel_id=1, source_target_pairs={{1,0},{2,1},{3,2},{4,3},{5,4},{6,5},{7,6},{9,8},{10,9},{11,10},{12... | collective-permute-start | bytes 4808 | tf_op jit(solution)/shard_map/ppermute | solution.py:34
  103.4 7.8 %collective-permute-start.14 = (f32[2,20,1,128]{3,2,1,0:T(1,128)S(1)}, f32[2,20,1,128]{3,2,1,0:T(1,128)S(1)}, u32[]{:S(2)}, u32[]{:S(2)}) collective-permute-start(f32[2,20,1,128]{3,2,1,0:T(1,128)S(1)} %get-tuple-element.57), channel_id=1, source_target_pairs={{0,8},{8,16},{16,24},{24,32},{32,40},{40,48},{48,56},{56,64},{64,7... | collective-permute-start | bytes 61448 | tf_op jit(solution)/shard_map/ppermute | solution.py:32
  105.3 7.2 %collective-permute-start.15 = (f32[2,20,1,128]{3,2,1,0:T(1,128)S(1)}, f32[2,20,1,128]{3,2,1,0:T(1,128)S(1)}, u32[]{:S(2)}, u32[]{:S(2)}) collective-permute-start(f32[2,20,1,128]{3,2,1,0:T(1,128)S(1)} %get-tuple-element.58), channel_id=1, source_target_pairs={{8,0},{16,8},{24,16},{32,24},{40,32},{48,40},{56,48},{64,56},{72,6... | collective-permute-start | bytes 61448 | tf_op jit(solution)/shard_map/ppermute | solution.py:34
  112.7 9.1 %collective-permute-start.16 = (f32[2,20,10,1]{3,2,1,0:T(8,128)S(1)}, f32[2,20,10,1]{3,2,1,0:T(8,128)S(1)}, u32[]{:S(2)}, u32[]{:S(2)}) collective-permute-start(f32[2,20,10,1]{3,2,1,0:T(8,128)S(1)} %get-tuple-element.37), channel_id=1, source_target_pairs={{0,1},{1,2},{2,3},{3,4},{4,5},{5,6},{6,7},{8,9},{9,10},{10,11},{11... | collective-permute-start | bytes 4808 | tf_op jit(solution)/shard_map/ppermute | solution.py:32
  116.6 13.0 %collective-permute-start.17 = (f32[2,20,10,1]{3,2,1,0:T(8,128)S(1)}, f32[2,20,10,1]{3,2,1,0:T(8,128)S(1)}, u32[]{:S(2)}, u32[]{:S(2)}) collective-permute-start(f32[2,20,10,1]{3,2,1,0:T(8,128)S(1)} %get-tuple-element.38), channel_id=1, source_target_pairs={{1,0},{2,1},{3,2},{4,3},{5,4},{6,5},{7,6},{9,8},{10,9},{11,10},{12... | collective-permute-start | bytes 4808 | tf_op jit(solution)/shard_map/ppermute | solution.py:34
  130.1 7.7 %collective-permute-start.18 = (f32[2,20,1,128]{3,2,1,0:T(1,128)S(1)}, f32[2,20,1,128]{3,2,1,0:T(1,128)S(1)}, u32[]{:S(2)}, u32[]{:S(2)}) collective-permute-start(f32[2,20,1,128]{3,2,1,0:T(1,128)S(1)} %get-tuple-element.53), channel_id=1, source_target_pairs={{0,8},{8,16},{16,24},{24,32},{32,40},{40,48},{48,56},{56,64},{64,7... | collective-permute-start | bytes 61448 | tf_op jit(solution)/shard_map/ppermute | solution.py:32
  132.0 7.2 %collective-permute-start.19 = (f32[2,20,1,128]{3,2,1,0:T(1,128)S(1)}, f32[2,20,1,128]{3,2,1,0:T(1,128)S(1)}, u32[]{:S(2)}, u32[]{:S(2)}) collective-permute-start(f32[2,20,1,128]{3,2,1,0:T(1,128)S(1)} %get-tuple-element.54), channel_id=1, source_target_pairs={{8,0},{16,8},{24,16},{32,24},{40,32},{48,40},{56,48},{64,56},{72,6... | collective-permute-start | bytes 61448 | tf_op jit(solution)/shard_map/ppermute | solution.py:34
  139.5 7.7 %collective-permute-start.20 = (f32[2,20,10,1]{3,2,1,0:T(8,128)S(1)}, f32[2,20,10,1]{3,2,1,0:T(8,128)S(1)}, u32[]{:S(2)}, u32[]{:S(2)}) collective-permute-start(f32[2,20,10,1]{3,2,1,0:T(8,128)S(1)} %get-tuple-element.35), channel_id=1, source_target_pairs={{0,1},{1,2},{2,3},{3,4},{4,5},{5,6},{6,7},{8,9},{9,10},{10,11},{11... | collective-permute-start | bytes 4808 | tf_op jit(solution)/shard_map/ppermute | solution.py:32
  141.4 13.6 %collective-permute-start.21 = (f32[2,20,10,1]{3,2,1,0:T(8,128)S(1)}, f32[2,20,10,1]{3,2,1,0:T(8,128)S(1)}, u32[]{:S(2)}, u32[]{:S(2)}) collective-permute-start(f32[2,20,10,1]{3,2,1,0:T(8,128)S(1)} %get-tuple-element.36), channel_id=1, source_target_pairs={{1,0},{2,1},{3,2},{4,3},{5,4},{6,5},{7,6},{9,8},{10,9},{11,10},{12... | collective-permute-start | bytes 4808 | tf_op jit(solution)/shard_map/ppermute | solution.py:34
  142.7 48.7 %copy-start.5 = (s32[1,1,256]{2,1,0:T(1,128)S(1)}, s32[1,1,256]{2,1,0:T(1,128)}, u32[]{:S(2)}) copy-start(s32[1,1,256]{2,1,0:T(1,128)} %param.20) | copy-start | bytes 3076
  142.7 48.7 %copy-start.6 = (f32[1,1,256]{2,1,0:T(1,128)S(1)}, f32[1,1,256]{2,1,0:T(1,128)}, u32[]{:S(2)}) copy-start(f32[1,1,256]{2,1,0:T(1,128)} %param.21) | copy-start | bytes 3076
  155.4 9.6 %collective-permute-start.22 = (f32[2,20,1,128]{3,2,1,0:T(1,128)S(1)}, f32[2,20,1,128]{3,2,1,0:T(1,128)S(1)}, u32[]{:S(2)}, u32[]{:S(2)}) collective-permute-start(f32[2,20,1,128]{3,2,1,0:T(1,128)S(1)} %get-tuple-element.49), channel_id=1, source_target_pairs={{0,8},{8,16},{16,24},{24,32},{32,40},{40,48},{48,56},{56,64},{64,7... | collective-permute-start | bytes 61448 | tf_op jit(solution)/shard_map/ppermute | solution.py:32
  157.3 7.7 %collective-permute-start.23 = (f32[2,20,1,128]{3,2,1,0:T(1,128)S(1)}, f32[2,20,1,128]{3,2,1,0:T(1,128)S(1)}, u32[]{:S(2)}, u32[]{:S(2)}) collective-permute-start(f32[2,20,1,128]{3,2,1,0:T(1,128)S(1)} %get-tuple-element.50), channel_id=1, source_target_pairs={{8,0},{16,8},{24,16},{32,24},{40,32},{48,40},{56,48},{64,56},{72,6... | collective-permute-start | bytes 61448 | tf_op jit(solution)/shard_map/ppermute | solution.py:34
  165.3 6.7 %collective-permute-start.24 = (f32[2,20,10,1]{3,2,1,0:T(8,128)S(1)}, f32[2,20,10,1]{3,2,1,0:T(8,128)S(1)}, u32[]{:S(2)}, u32[]{:S(2)}) collective-permute-start(f32[2,20,10,1]{3,2,1,0:T(8,128)S(1)} %get-tuple-element.33), channel_id=1, source_target_pairs={{0,1},{1,2},{2,3},{3,4},{4,5},{5,6},{6,7},{8,9},{9,10},{10,11},{11... | collective-permute-start | bytes 4808 | tf_op jit(solution)/shard_map/ppermute | solution.py:32
  166.8 13.0 %collective-permute-start.25 = (f32[2,20,10,1]{3,2,1,0:T(8,128)S(1)}, f32[2,20,10,1]{3,2,1,0:T(8,128)S(1)}, u32[]{:S(2)}, u32[]{:S(2)}) collective-permute-start(f32[2,20,10,1]{3,2,1,0:T(8,128)S(1)} %get-tuple-element.34), channel_id=1, source_target_pairs={{1,0},{2,1},{3,2},{4,3},{5,4},{6,5},{7,6},{9,8},{10,9},{11,10},{12... | collective-permute-start | bytes 4808 | tf_op jit(solution)/shard_map/ppermute | solution.py:34
